TPU v7x, 32 devices: a whole 2x2x4 slice. The times are simulated.
32 devices in a mesh: orb: 8 (over z, core), spx: 4 (over y, x).
Axes of the slice: x: 2, y: 2, z: 4, core: 2. Of those that a mesh axis runs over, the one named last changes fastest.
Arguments:
- weights: float32 [32768], P('orb'), may hold values from 0.25 to 2
- losvd: bfloat16 [32768, 32, 64], P('orb', 'spx'), may hold values from 0 to 0.015625
- occupancy: int32 [256, 32], P('orb', 'spx'), may hold values 0 or 1
- template_of: int32 [32768], P('orb'), may hold values from 0 to 255
- templates: bfloat16 [256, 4160], P('orb'), may hold values from -0.046875 to 0.046875
- observed: float32 [32, 4096], P('spx'), may hold values from -6 to 6
- inv_sigma: float32 [32, 4096], P('spx'), may hold values from 0.5 to 2
Outputs:
- weights_next: float32 [32768], P('orb')
- residual: float32 [32, 4096], P('spx')
All inputs are finite; a program needn't handle non-finite values. No bound on the sum of `occupancy` on one device may be relied on, other than what follows from the above.
Results may differ from a plain program's by a relative error of at most 0.0005.
Values may be sent and summed in bfloat16 or wider, within the bound.
A program may use at most 128 MiB of HBM per device.

v0:
```python
import functools
import jax
import jax.numpy as jnp
from jax import lax
from jax.experimental import pallas as pl
from jax.experimental.pallas import tpu as pltpu
from jax.sharding import PartitionSpec as P

step_size = 0.5
MESH = pl.DeviceIdType.MESH
f32, bf16, i32 = jnp.float32, jnp.bfloat16, jnp.int32
NT = (((1,), (1,)), ((), ()))
NN = (((1,), (0,)), ((), ()))
fine = 8


def dot(a, b, dims):
    return lax.dot_general(a, b, dims, preferred_element_type=f32)


def iota(shape, axis):
    return lax.broadcasted_iota(i32, shape, axis)


def kernel(n, m, velocity_bins, block,
           w_ref, lt_hbm, occ_ref, tid_ref, t_ref, obs_ref, inv_ref,
           out_w, out_res,
           lt, part, pair, mixin, hank, model, modelin, resid, table, grads,
           load_sem, pair_sem, mix_send, mix_recv, mod_send, mod_recv, res_send, res_recv,
           tab_send, tab_recv, fwd_send, grad_send, grad_recv):
    chunks, rows, oc = lt.shape
    spaxels, waves = obs_ref.shape
    own, twaves = t_ref.shape
    coarse = velocity_bins // fine
    wide = hank.shape[1]
    total = n * own
    chips = n // 2
    me = lax.axis_index("orb")
    mine = lax.axis_index("spx")
    core, chip = lax.rem(me, 2), lax.div(me, 2)
    sibling = chip * 2 + (1 - core)

    def load(c):
        return pltpu.make_async_copy(
            lt_hbm.at[:, pl.ds(pl.multiple_of(c * oc, oc), oc)], lt.at[c], load_sem.at[c])

    for c in range(chunks):
        load(c).start()

    barrier = pltpu.get_barrier_semaphore()
    for j in range(1, n):
        pl.semaphore_signal(barrier, inc=1, device_id={"orb": lax.rem(me + j, n)}, device_id_type=MESH)
    for j in range(1, m):
        pl.semaphore_signal(barrier, inc=1, device_id={"spx": lax.rem(mine + j, m)}, device_id_type=MESH)

    four = (2, chips, own, oc)
    row_template = ((iota(four, 1) * 2 + iota(four, 0)) * own + iota(four, 2)).reshape(total, oc)
    occupied = occ_ref[...].astype(f32).astype(bf16)
    blocks = occupied.shape[1]
    part[...] = jnp.zeros_like(part)

    def mix(c, carry):
        load(c).wait()
        at = pl.ds(pl.multiple_of(c * oc, oc), oc)
        place = c * oc + iota((blocks, oc), 1) - iota((blocks, oc), 0) * block
        expand = jnp.where((place >= 0) & (place < block), 1.0, 0.0).astype(bf16)
        mask = dot(occupied, expand, NN).astype(bf16)
        for s in range(spaxels):
            band = pl.ds(s * velocity_bins, velocity_bins)
            lt[c, band, :] = lt[c, band, :] * mask[s : s + 1, :]
        weight = w_ref[:, at].astype(bf16).astype(f32)
        assign = jnp.where(row_template == tid_ref[:, at], weight, 0.0).astype(bf16)
        part[...] += dot(assign, lt[c], NT).reshape(part.shape)
        return carry

    lax.fori_loop(0, chunks, mix, 0)

    pl.semaphore_wait(barrier, n - 1 + m - 1)

    swap = pltpu.make_async_remote_copy(
        src_ref=part.at[1 - core], dst_ref=pair, send_sem=pair_sem.at[0], recv_sem=pair_sem.at[1],
        device_id={"orb": sibling}, device_id_type=MESH)
    swap.start()

    padded = jnp.concatenate(
        [t_ref[...].astype(f32), jnp.zeros((own, wide - twaves), f32)], axis=1)
    for q in range(0, coarse, 2):
        pieces = [pltpu.roll(padded, (wide - fine * k) % wide, 1) if k else padded for k in (q, q + 1)]
        hank[pl.ds(q * own, 2 * own), :] = jnp.concatenate(pieces, axis=0).astype(bf16)
    lane = iota((8, rows), 1)
    lane_coarse = lax.div(lax.rem(lane, velocity_bins), fine)
    cube = (fine, spaxels, rows)
    select = jnp.where(
        iota(cube, 1) * velocity_bins + lane_coarse[None, :1, :] * fine + iota(cube, 0) == iota(cube, 2),
        1.0, 0.0).reshape(fine * spaxels, rows).astype(bf16)
    layers = (coarse, own, rows)
    keep = iota(layers, 0) == lane_coarse[None, :1, :]

    swap.wait()
    part[core] = part[core] + pair[...]

    def to_chip(j):
        other = lax.rem(chip + j, chips)
        return pltpu.make_async_remote_copy(
            src_ref=part.at[core, other], dst_ref=mixin.at[chip],
            send_sem=mix_send.at[j], recv_sem=mix_recv.at[chip],
            device_id={"orb": other * 2 + core}, device_id_type=MESH)

    def arrived(ref, sems, source):
        pltpu.make_async_copy(ref.at[source], ref.at[source], sems.at[source]).wait()

    for j in range(1, chips):
        to_chip(j).start()
    mixture = part[core, chip]
    for j in range(1, chips):
        source = lax.rem(chip + j, chips)
        arrived(mixin, mix_recv, source)
        mixture = mixture + mixin[source]

    high = mixture.astype(bf16)
    low = (mixture - high.astype(f32)).astype(bf16)
    columns = []
    for half in (high, low):
        spread = jnp.where(keep, half.astype(f32)[None], 0.0).reshape(coarse * own, rows).astype(bf16)
        columns.append(dot(select, spread, NT))
    both = jnp.concatenate(columns, axis=0).astype(bf16)
    product = dot(both, hank[...], NN)
    tall = fine * spaxels
    product = product[:tall] + product[tall:]
    sums = product[:spaxels]
    for r in range(1, fine):
        sums = sums + pltpu.roll(product[r * spaxels : (r + 1) * spaxels], wide - r, 1)
    span = waves // n
    for d in range(n):
        model[d] = sums[:, d * span : (d + 1) * span]

    def to_owner(j):
        other = lax.rem(me + j, n)
        return pltpu.make_async_remote_copy(
            src_ref=model.at[other], dst_ref=modelin.at[me],
            send_sem=mod_send.at[j], recv_sem=mod_recv.at[me],
            device_id={"orb": other}, device_id_type=MESH)

    def to_all(j):
        other = lax.rem(me + j, n)
        return pltpu.make_async_remote_copy(
            src_ref=resid.at[me], dst_ref=resid.at[me],
            send_sem=res_send.at[j], recv_sem=res_recv.at[me],
            device_id={"orb": other}, device_id_type=MESH)

    for j in range(1, n):
        to_owner(j).start()
    whole = model[me]
    for j in range(1, n):
        source = lax.rem(me + j, n)
        arrived(modelin, mod_recv, source)
        whole = whole + modelin[source]
    at = pl.ds(pl.multiple_of(me * span, span), span)
    resid[me] = (whole - obs_ref[:, at]) * inv_ref[:, at]
    for j in range(1, n):
        to_all(j).start()
    for j in range(1, n):
        arrived(resid, res_recv, lax.rem(me + j, n))
    residual = jnp.concatenate([resid[d] for d in range(n)], axis=1)
    out_res[...] = residual
    scaled = (residual * inv_ref[...]).astype(bf16).astype(f32)
    scaled = jnp.concatenate([scaled, jnp.zeros((spaxels, wide - waves), f32)], axis=1)
    shifted = jnp.concatenate(
        [pltpu.roll(scaled, r, 1) if r else scaled for r in range(fine)], axis=0).astype(bf16)
    response = dot(hank[...], shifted, NT).astype(bf16)
    laid = dot(response, select, NN).reshape(layers)
    table[me] = jnp.sum(jnp.where(keep, laid, 0.0), axis=0).astype(bf16)

    def to_peer(j):
        other = lax.rem(chip + j, chips)
        return pltpu.make_async_remote_copy(
            src_ref=table.at[me], dst_ref=table.at[me],
            send_sem=tab_send.at[j], recv_sem=tab_recv.at[me],
            device_id={"orb": other * 2 + core}, device_id_type=MESH)

    def forward(j):
        source = lax.rem(chip + j, chips) * 2 + core
        return pltpu.make_async_remote_copy(
            src_ref=table.at[source], dst_ref=table.at[source],
            send_sem=fwd_send.at[j], recv_sem=tab_recv.at[source],
            device_id={"orb": sibling}, device_id_type=MESH)

    for j in range(1, chips):
        to_peer(j).start()
    forward(0).start()
    for j in range(1, chips):
        arrived(table, tab_recv, lax.rem(chip + j, chips) * 2 + core)
        forward(j).start()
    for j in range(chips):
        arrived(table, tab_recv, lax.rem(chip + j, chips) * 2 + 1 - core)

    responses = jnp.concatenate([table[d].astype(f32) for d in range(n)], axis=0).astype(bf16)
    shape = (total, oc)

    def grad(c, carry):
        at = pl.ds(pl.multiple_of(c * oc, oc), oc)
        scores = dot(responses, lt[c], NN)
        grads[mine, :, at] = jnp.sum(
            jnp.where(iota(shape, 0) == tid_ref[:, at], scores, 0.0), axis=0, keepdims=True)
        return carry

    lax.fori_loop(0, chunks, grad, 0)

    def to_group(j):
        return pltpu.make_async_remote_copy(
            src_ref=grads.at[mine], dst_ref=grads.at[mine],
            send_sem=grad_send.at[j], recv_sem=grad_recv.at[mine],
            device_id={"spx": lax.rem(mine + j, m)}, device_id_type=MESH)

    for j in range(1, m):
        to_group(j).start()
    for j in range(1, m):
        arrived(grads, grad_recv, lax.rem(mine + j, m))
    gradient = grads[0]
    for i in range(1, m):
        gradient = gradient + grads[i]
    out_w[...] = jnp.maximum(w_ref[...] - step_size * gradient, 0.0)

    for j in range(1, chips):
        to_chip(j).wait_send()
        to_peer(j).wait_send()
    for j in range(chips):
        forward(j).wait_send()
    for j in range(1, n):
        to_owner(j).wait_send()
        to_all(j).wait_send()
    for j in range(1, m):
        to_group(j).wait_send()


def local(weights, losvd, occupancy, template_of, templates, observed, inv_sigma):
    orbits, spaxels, velocity_bins = losvd.shape
    blocks = occupancy.shape[0]
    n, m = lax.axis_size("orb"), lax.axis_size("spx")
    own, twaves = templates.shape
    waves = observed.shape[1]
    rows = spaxels * velocity_bins
    oc = min(512, orbits)
    chunks = orbits // oc
    wide = -(-twaves // 128) * 128
    chips = n // 2
    coarse = velocity_bins // fine
    dma = pltpu.SemaphoreType.DMA
    vmem = pl.BlockSpec(memory_space=pltpu.VMEM)
    out_w, out_res = pl.pallas_call(
        functools.partial(kernel, n, m, velocity_bins, orbits // blocks),
        out_shape=(jax.ShapeDtypeStruct((1, orbits), f32), jax.ShapeDtypeStruct((spaxels, waves), f32)),
        in_specs=[vmem, pl.BlockSpec(memory_space=pl.ANY)] + [vmem] * 5,
        out_specs=(vmem, vmem),
        scratch_shapes=[
            pltpu.VMEM((chunks, rows, oc), bf16),
            pltpu.VMEM((2, chips, own, rows), f32),
            pltpu.VMEM((chips, own, rows), f32),
            pltpu.VMEM((chips, own, rows), f32),
            pltpu.VMEM((coarse * own, wide), bf16),
            pltpu.VMEM((n, spaxels, waves // n), f32),
            pltpu.VMEM((n, spaxels, waves // n), f32),
            pltpu.VMEM((n, spaxels, waves // n), f32),
            pltpu.VMEM((n, own, rows), bf16),
            pltpu.VMEM((m, 1, orbits), f32),
            dma((chunks,)), dma((2,)),
            dma((chips,)), dma((chips,)),
            dma((n,)), dma((n,)), dma((n,)), dma((n,)),
            dma((chips,)), dma((n,)), dma((chips,)),
            dma((m,)), dma((m,)),
        ],
        compiler_params=pltpu.CompilerParams(
            collective_id=0, has_side_effects=True, vmem_limit_bytes=48 * 2**20),
    )(
        weights.reshape(1, orbits),
        jnp.transpose(losvd, (1, 2, 0)).reshape(rows, orbits),
        occupancy.T,
        template_of.reshape(1, orbits),
        templates, observed, inv_sigma,
    )
    return out_w.reshape(orbits), out_res


def solution(mesh):
    placed = (
        P("orb"),
        P("orb", "spx", None),
        P("orb", "spx"),
        P("orb"),
        P("orb", None),
        P("spx", None),
        P("spx", None),
    )
    return jax.shard_map(
        local, mesh=mesh, in_specs=placed, out_specs=(P("orb"), P("spx", None)), check_vma=False
    )
```

profile of v0, /device:TPU:0, one launch (start us, length us, event | category | flops | bytes accessed | tf_op | source)
XLA Modules:
  0.0 47.6 jit_solution(11578300411546883293)
XLA Ops:
  0.6 0.0 copy-start
  0.6 2.2 %copy-done = bf16[4096,8,64]{0,2,1:T(8,128)(2,1)S(1)} copy-done((bf16[4096,8,64]{0,2,1:T(8,128)(2,1)S(1)}, bf16[4096,8,64]{0,2,1:T(8,128)(2,1)}, u32[]{:S(2)}) %copy-start) | copy-done | bytes 4194328
  2.8 0.0 copy-start.1
  2.8 1.0 %copy-done.1 = bf16[32,4160]{1,0:T(8,128)(2,1)S(1)} copy-done((bf16[32,4160]{1,0:T(8,128)(2,1)S(1)}, bf16[32,4160]{1,0:T(8,128)(2,1)}, u32[]{:S(2)}) %copy-start.1) | copy-done | bytes 266264
  3.8 0.0 copy-start.2
  3.8 0.9 %copy-done.2 = f32[8,4096]{1,0:T(8,128)S(1)} copy-done((f32[8,4096]{1,0:T(8,128)S(1)}, f32[8,4096]{1,0:T(8,128)}, u32[]{:S(2)}) %copy-start.2) | copy-done | bytes 131096
  4.7 0.0 copy-start.3
  4.7 0.9 %copy-done.3 = f32[8,4096]{1,0:T(8,128)S(1)} copy-done((f32[8,4096]{1,0:T(8,128)S(1)}, f32[8,4096]{1,0:T(8,128)}, u32[]{:S(2)}) %copy-start.3) | copy-done | bytes 131096
  5.6 0.0 copy-start.4
  5.6 0.7 %copy-done.4 = f32[4096]{0:T(1024)S(1)} copy-done((f32[4096]{0:T(1024)S(1)}, f32[4096]{0:T(1024)}, u32[]{:S(2)}) %copy-start.4) | copy-done | bytes 16408
  6.3 0.0 copy-start.5
  6.3 0.7 %copy-done.5 = s32[4096]{0:T(1024)S(1)} copy-done((s32[4096]{0:T(1024)S(1)}, s32[4096]{0:T(1024)}, u32[]{:S(2)}) %copy-start.5) | copy-done | bytes 16408
  7.0 0.0 copy-start.6
  7.0 0.7 %copy-done.6 = s32[32,8]{0,1:T(8,128)S(1)} copy-done((s32[32,8]{0,1:T(8,128)S(1)}, s32[32,8]{0,1:T(8,128)}, u32[]{:S(2)}) %copy-start.6) | copy-done | bytes 1048
  7.7 38.6 %shard_map.86 = (f32[1,4096]{1,0:T(1,128)S(1)}, f32[8,4096]{1,0:T(8,128)S(1)}) custom-call(f32[1,4096]{1,0:T(1,128)S(1)} %bitcast.8, bf16[512,4096]{1,0:T(8,128)(2,1)S(1)} %bitcast.7, s32[8,32]{1,0:T(8,128)S(1)} %bitcast.11, s32[1,4096]{1,0:T(1,128)S(1)} %bitcast.9, bf16[32,4160]{1,0:T(8,128)(2,1)S(1)} %copy-done.1, f32[8,4096]{1,0:T(8,128)S(1)} %copy-done.2, ...), custom_call_target="tpu_custom_call" | custom-call | tf_op jit(solution)/shard_map/pallas_call | solution.py:250
  46.4 0.6 %copy.11 = f32[4096]{0:T(1024)} copy(f32[4096]{0:T(1024)S(1)} %bitcast.10) | data formatting | bytes 32768
  47.0 0.7 %copy.12 = f32[8,4096]{1,0:T(8,128)} copy(f32[8,4096]{1,0:T(8,128)S(1)} %get-tuple-element.9) | data formatting | bytes 262144
Async XLA Ops:
  0.6 2.2 %copy-start = (bf16[4096,8,64]{0,2,1:T(8,128)(2,1)S(1)}, bf16[4096,8,64]{0,2,1:T(8,128)(2,1)}, u32[]{:S(2)}) copy-start(bf16[4096,8,64]{0,2,1:T(8,128)(2,1)} %param.8) | copy-start | bytes 12582916
  2.8 1.0 %copy-start.1 = (bf16[32,4160]{1,0:T(8,128)(2,1)S(1)}, bf16[32,4160]{1,0:T(8,128)(2,1)}, u32[]{:S(2)}) copy-start(bf16[32,4160]{1,0:T(8,128)(2,1)} %t_ref.1) | copy-start | bytes 798724
  3.8 0.9 %copy-start.2 = (f32[8,4096]{1,0:T(8,128)S(1)}, f32[8,4096]{1,0:T(8,128)}, u32[]{:S(2)}) copy-start(f32[8,4096]{1,0:T(8,128)} %obs_ref.1) | copy-start | bytes 393220
  4.7 0.9 %copy-start.3 = (f32[8,4096]{1,0:T(8,128)S(1)}, f32[8,4096]{1,0:T(8,128)}, u32[]{:S(2)}) copy-start(f32[8,4096]{1,0:T(8,128)} %inv_ref.1) | copy-start | bytes 393220
  5.6 0.7 %copy-start.4 = (f32[4096]{0:T(1024)S(1)}, f32[4096]{0:T(1024)}, u32[]{:S(2)}) copy-start(f32[4096]{0:T(1024)} %param.7) | copy-start | bytes 49156
  6.3 0.7 %copy-start.5 = (s32[4096]{0:T(1024)S(1)}, s32[4096]{0:T(1024)}, u32[]{:S(2)}) copy-start(s32[4096]{0:T(1024)} %param.10) | copy-start | bytes 49156
  7.0 0.7 %copy-start.6 = (s32[32,8]{0,1:T(8,128)S(1)}, s32[32,8]{0,1:T(8,128)}, u32[]{:S(2)}) copy-start(s32[32,8]{0,1:T(8,128)} %param.9) | copy-start | bytes 3076
where the time goes:
time: 48 us; the launch traced here: 47.6 us
  Pallas kernels  38.6 us (80%)
  local copies, waits for them, and re-layouts  8.32 us (17%)
  between operations  0.66 us (1%)
    pallas_call x1, Pallas kernels, local(): pl.pallas_call(functools.partial(kernel, n, m, velocity_bins, orbits // b...  38.6 us
    unnamed x16, local copies, waits for them, and re-layouts  8.32 us

commit v1 on v0

v1 whole, which is shorter than its diff:
```python
import functools
import jax
import jax.numpy as jnp
from jax import lax
from jax.experimental import pallas as pl
from jax.experimental.pallas import tpu as pltpu
from jax.sharding import PartitionSpec as P

step_size = 0.5
MESH = pl.DeviceIdType.MESH
f32, bf16, i32 = jnp.float32, jnp.bfloat16, jnp.int32
NT = (((1,), (1,)), ((), ()))
NN = (((1,), (0,)), ((), ()))
fine = 8


def dot(a, b, dims):
    return lax.dot_general(a, b, dims, preferred_element_type=f32)


def iota(shape, axis):
    return lax.broadcasted_iota(i32, shape, axis)


def kernel(n, m, velocity_bins, block,
           w_hbm, lt_hbm, occ_hbm, tid_hbm, t_hbm, obs_hbm, inv_hbm,
           out_w, out_res,
           w_ref, occ_ref, tid_ref, t_ref, obs_ref, inv_ref,
           lt, masks, assigned, part, pair, mixin, hank, model, modelin, resid, table, grads,
           small_sem, load_sem, pair_send, pair_recv, mix_send, mix_recv, mod_send, mod_recv,
           res_send, res_recv, tab_send, tab_recv, fwd_send, grad_send, grad_recv):
    halves, chunks, rows, oc = lt.shape
    spaxels, waves = obs_ref.shape
    own, twaves = t_ref.shape
    coarse = velocity_bins // fine
    wide = hank.shape[1]
    total = n * own
    chips = n // 2
    span = waves // n
    reach = span + wide - waves
    tall = fine * spaxels
    groups = grads.shape[0]
    me = lax.axis_index("orb")
    mine = lax.axis_index("spx")
    core, chip = lax.rem(me, 2), lax.div(me, 2)
    sibling = chip * 2 + (1 - core)

    def load(h, c):
        return pltpu.make_async_copy(
            lt_hbm.at[pl.ds(h * rows, rows), pl.ds(pl.multiple_of(c * oc, oc), oc)],
            lt.at[h, c], load_sem.at[h, c])

    small = [
        pltpu.make_async_copy(source, target, small_sem.at[i])
        for i, (source, target) in enumerate(
            ((occ_hbm, occ_ref), (tid_hbm, tid_ref), (w_hbm, w_ref),
             (t_hbm, t_ref), (obs_hbm, obs_ref), (inv_hbm, inv_ref)))
    ]
    for copy in small[:3]:
        copy.start()
    for h in range(halves):
        for c in range(chunks):
            load(h, c).start()
    for copy in small[3:]:
        copy.start()

    barrier = pltpu.get_barrier_semaphore()
    for j in range(1, n):
        pl.semaphore_signal(barrier, inc=1, device_id={"orb": lax.rem(me + j, n)}, device_id_type=MESH)
    for j in range(1, m):
        pl.semaphore_signal(barrier, inc=1, device_id={"spx": lax.rem(mine + j, m)}, device_id_type=MESH)

    four = (2, chips, own, oc)
    row_template = ((iota(four, 1) * 2 + iota(four, 0)) * own + iota(four, 2)).reshape(total, oc)
    part[...] = jnp.zeros_like(part)
    for copy in small[:3]:
        copy.wait()
    occupied = occ_ref[...].astype(f32).astype(bf16)
    blocks = occupied.shape[1]

    def cover(h, c, mask):
        for s in range(rows // velocity_bins):
            band = pl.ds(s * velocity_bins, velocity_bins)
            row = h * (rows // velocity_bins) + s
            lt[h, c, band, :] = lt[h, c, band, :] * mask[row : row + 1, :]

    def mix_first(c, carry):
        at = pl.ds(pl.multiple_of(c * oc, oc), oc)
        place = c * oc + iota((blocks, oc), 1) - iota((blocks, oc), 0) * block
        expand = jnp.where((place >= 0) & (place < block), 1.0, 0.0).astype(bf16)
        mask = dot(occupied, expand, NN)
        masks[c] = mask
        weight = w_ref[:, at].astype(bf16).astype(f32)
        assign = jnp.where(row_template == tid_ref[:, at], weight, 0.0).astype(bf16)
        assigned[c] = assign
        load(0, c).wait()
        cover(0, c, mask.astype(bf16))
        part[0] += dot(assign, lt[0, c], NT).reshape(part.shape[1:])
        return carry

    lax.fori_loop(0, chunks, mix_first, 0)

    def swap(h):
        return pltpu.make_async_remote_copy(
            src_ref=part.at[h, 1 - core], dst_ref=pair.at[h],
            send_sem=pair_send.at[h], recv_sem=pair_recv.at[h],
            device_id={"orb": sibling}, device_id_type=MESH)

    def to_chip(h, j):
        other = lax.rem(chip + j, chips)
        return pltpu.make_async_remote_copy(
            src_ref=part.at[h, core, other], dst_ref=mixin.at[h, chip],
            send_sem=mix_send.at[h, j], recv_sem=mix_recv.at[h, chip],
            device_id={"orb": other * 2 + core}, device_id_type=MESH)

    def arrived(ref, sem):
        pltpu.make_async_copy(ref, ref, sem).wait()

    pl.semaphore_wait(barrier, n - 1 + m - 1)
    swap(0).start()

    def mix(h):
        def step(c, carry):
            load(h, c).wait()
            cover(h, c, masks[c].astype(bf16))
            part[h] += dot(assigned[c], lt[h, c], NT).reshape(part.shape[1:])
            return carry

        lax.fori_loop(0, chunks, step, 0)

    def spread(h):
        swap(h).wait()
        part[h, core] = part[h, core] + pair[h]
        for j in range(1, chips):
            to_chip(h, j).start()

    for h in range(1, halves):
        mix(h)
        swap(h).start()
        spread(h - 1)

    for copy in small[3:]:
        copy.wait()
    padded = jnp.concatenate(
        [t_ref[...].astype(f32), jnp.zeros((own, wide - twaves), f32)], axis=1)

    def fold(q):
        pieces = [pltpu.roll(padded, (wide - fine * k) % wide, 1) if k else padded for k in (q, q + 1)]
        hank[pl.ds(q * own, 2 * own), :] = jnp.concatenate(pieces, axis=0).astype(bf16)

    fold(0)
    spread(halves - 1)
    for q in range(2, coarse, 2):
        fold(q)
    lane_coarse = lax.div(lax.rem(iota((8, rows), 1), velocity_bins), fine)
    cube = (fine, spaxels, rows)
    selects = [
        jnp.where(
            (iota(cube, 1) - h * (rows // velocity_bins)) * velocity_bins
            + lane_coarse[None, :1, :] * fine + iota(cube, 0) == iota(cube, 2),
            1.0, 0.0).reshape(tall, rows).astype(bf16)
        for h in range(halves)
    ]
    layers = (coarse, own, rows)
    keep = iota(layers, 0) == lane_coarse[None, :1, :]

    both = None
    for h in range(halves):
        mixture = part[h, core, chip]
        for j in range(1, chips):
            source = lax.rem(chip + j, chips)
            arrived(mixin.at[h, source], mix_recv.at[h, source])
            mixture = mixture + mixin[h, source]
        high = mixture.astype(bf16)
        low = (mixture - high.astype(f32)).astype(bf16)
        columns = []
        for piece in (high, low):
            layered = jnp.where(keep, piece.astype(f32)[None], 0.0).reshape(coarse * own, rows).astype(bf16)
            columns.append(dot(selects[h], layered, NT))
        found = jnp.concatenate(columns, axis=0)
        both = found if both is None else both + found
    both = both.astype(bf16)

    def to_owner(j):
        other = lax.rem(me + j, n)
        return pltpu.make_async_remote_copy(
            src_ref=model.at[other], dst_ref=modelin.at[me],
            send_sem=mod_send.at[j], recv_sem=mod_recv.at[me],
            device_id={"orb": other}, device_id_type=MESH)

    def to_all(j):
        other = lax.rem(me + j, n)
        return pltpu.make_async_remote_copy(
            src_ref=resid.at[me], dst_ref=resid.at[me],
            send_sem=res_send.at[j], recv_sem=res_recv.at[me],
            device_id={"orb": other}, device_id_type=MESH)

    for j in range(1, n + 1):
        other = lax.rem(me + j, n)
        product = dot(both, hank[:, pl.ds(pl.multiple_of(other * span, span), reach)], NN)
        product = product[:tall] + product[tall:]
        sums = product[:spaxels]
        for r in range(1, fine):
            sums = sums + pltpu.roll(product[r * spaxels : (r + 1) * spaxels], reach - r, 1)
        model[other] = sums[:, :span]
        if j < n:
            to_owner(j).start()
    whole = model[me]
    for j in range(1, n):
        source = lax.rem(me + j, n)
        arrived(modelin.at[source], mod_recv.at[source])
        whole = whole + modelin[source]
    at = pl.ds(pl.multiple_of(me * span, span), span)
    resid[me] = (whole - obs_ref[:, at]) * inv_ref[:, at]
    for j in range(1, n):
        to_all(j).start()

    response = jnp.zeros((coarse * own, tall), f32)
    for j in range(n):
        source = lax.rem(me + j, n)
        if j:
            arrived(resid.at[source], res_recv.at[source])
        at = pl.ds(pl.multiple_of(source * span, span), span)
        piece = resid[source]
        out_res[:, at] = piece
        scaled = (piece * inv_ref[:, at]).astype(bf16).astype(f32)
        scaled = jnp.concatenate([scaled, jnp.zeros((spaxels, reach - span), f32)], axis=1)
        shifted = jnp.concatenate(
            [pltpu.roll(scaled, r, 1) if r else scaled for r in range(fine)], axis=0).astype(bf16)
        response = response + dot(
            hank[:, pl.ds(pl.multiple_of(source * span, span), reach)], shifted, NT)
    response = response.astype(bf16)
    for h in range(halves):
        laid = dot(response, selects[h], NN).reshape(layers)
        table[me, :, h * rows : (h + 1) * rows] = jnp.sum(
            jnp.where(keep, laid, 0.0), axis=0).astype(bf16)

    def to_peer(j):
        other = lax.rem(chip + j, chips)
        return pltpu.make_async_remote_copy(
            src_ref=table.at[me], dst_ref=table.at[me],
            send_sem=tab_send.at[j], recv_sem=tab_recv.at[me],
            device_id={"orb": other * 2 + core}, device_id_type=MESH)

    def forward(j):
        source = lax.rem(chip + j, chips) * 2 + core
        return pltpu.make_async_remote_copy(
            src_ref=table.at[source], dst_ref=table.at[source],
            send_sem=fwd_send.at[j], recv_sem=tab_recv.at[source],
            device_id={"orb": sibling}, device_id_type=MESH)

    for j in range(1, chips):
        to_peer(j).start()
    forward(0).start()
    for j in range(1, chips):
        source = lax.rem(chip + j, chips) * 2 + core
        arrived(table.at[source], tab_recv.at[source])
        forward(j).start()
    for j in range(chips):
        source = lax.rem(chip + j, chips) * 2 + 1 - core
        arrived(table.at[source], tab_recv.at[source])

    responses = jnp.concatenate([table[d].astype(f32) for d in range(n)], axis=0).astype(bf16)
    shape = (total, oc)

    def to_group(g, j):
        return pltpu.make_async_remote_copy(
            src_ref=grads.at[g, mine], dst_ref=grads.at[g, mine],
            send_sem=grad_send.at[g, j], recv_sem=grad_recv.at[g, mine],
            device_id={"spx": lax.rem(mine + j, m)}, device_id_type=MESH)

    each = chunks // groups
    for g in range(groups):
        def grad(k, carry, g=g):
            c = g * each + k
            at = pl.ds(pl.multiple_of(c * oc, oc), oc)
            scores = dot(responses[:, :rows], lt[0, c], NN)
            for h in range(1, halves):
                scores = scores + dot(responses[:, h * rows : (h + 1) * rows], lt[h, c], NN)
            grads[g, mine, :, pl.ds(pl.multiple_of(k * oc, oc), oc)] = jnp.sum(
                jnp.where(iota(shape, 0) == tid_ref[:, at], scores, 0.0), axis=0, keepdims=True)
            return carry

        lax.fori_loop(0, each, grad, 0)
        for j in range(1, m):
            to_group(g, j).start()
    for g in range(groups):
        for j in range(1, m):
            source = lax.rem(mine + j, m)
            arrived(grads.at[g, source], grad_recv.at[g, source])
        gradient = grads[g, 0]
        for i in range(1, m):
            gradient = gradient + grads[g, i]
        at = slice(g * each * oc, (g + 1) * each * oc)
        out_w[:, at] = jnp.maximum(w_ref[:, at] - step_size * gradient, 0.0)

    for h in range(halves):
        for j in range(1, chips):
            to_chip(h, j).wait_send()
    for j in range(1, chips):
        to_peer(j).wait_send()
    for j in range(chips):
        forward(j).wait_send()
    for j in range(1, n):
        to_owner(j).wait_send()
        to_all(j).wait_send()
    for g in range(groups):
        for j in range(1, m):
            to_group(g, j).wait_send()


def local(weights, losvd, occupancy, template_of, templates, observed, inv_sigma):
    orbits, spaxels, velocity_bins = losvd.shape
    blocks = occupancy.shape[0]
    n, m = lax.axis_size("orb"), lax.axis_size("spx")
    own, twaves = templates.shape
    waves = observed.shape[1]
    rows = spaxels * velocity_bins
    oc = min(512, orbits)
    chunks = orbits // oc
    wide = waves + -(-(twaves - waves) // 128) * 128
    halves = groups = 2
    half = rows // halves
    chips = n // 2
    coarse = velocity_bins // fine
    dma = pltpu.SemaphoreType.DMA
    vmem = pl.BlockSpec(memory_space=pltpu.VMEM)
    out_w, out_res = pl.pallas_call(
        functools.partial(kernel, n, m, velocity_bins, orbits // blocks),
        out_shape=(jax.ShapeDtypeStruct((1, orbits), f32), jax.ShapeDtypeStruct((spaxels, waves), f32)),
        in_specs=[pl.BlockSpec(memory_space=pltpu.HBM)] * 7,
        out_specs=(vmem, vmem),
        scratch_shapes=[
            pltpu.VMEM((1, orbits), f32),
            pltpu.VMEM((spaxels, blocks), i32),
            pltpu.VMEM((1, orbits), i32),
            pltpu.VMEM((own, twaves), bf16),
            pltpu.VMEM((spaxels, waves), f32),
            pltpu.VMEM((spaxels, waves), f32),
            pltpu.VMEM((halves, chunks, half, oc), bf16),
            pltpu.VMEM((chunks, spaxels, oc), f32),
            pltpu.VMEM((chunks, n * own, oc), bf16),
            pltpu.VMEM((halves, 2, chips, own, half), f32),
            pltpu.VMEM((halves, chips, own, half), f32),
            pltpu.VMEM((halves, chips, own, half), f32),
            pltpu.VMEM((coarse * own, wide), bf16),
            pltpu.VMEM((n, spaxels, waves // n), f32),
            pltpu.VMEM((n, spaxels, waves // n), f32),
            pltpu.VMEM((n, spaxels, waves // n), f32),
            pltpu.VMEM((n, own, rows), bf16),
            pltpu.VMEM((groups, m, 1, orbits // groups), f32),
            dma((6,)), dma((halves, chunks)), dma((halves,)), dma((halves,)),
            dma((halves, chips)), dma((halves, chips)),
            dma((n,)), dma((n,)), dma((n,)), dma((n,)),
            dma((chips,)), dma((n,)), dma((chips,)),
            dma((groups, m)), dma((groups, m)),
        ],
        compiler_params=pltpu.CompilerParams(
            collective_id=0, has_side_effects=True, vmem_limit_bytes=48 * 2**20),
    )(
        weights.reshape(1, orbits),
        jnp.transpose(losvd, (1, 2, 0)).reshape(rows, orbits),
        occupancy.T,
        template_of.reshape(1, orbits),
        templates, observed, inv_sigma,
    )
    return out_w.reshape(orbits), out_res


def solution(mesh):
    placed = (
        P("orb"),
        P("orb", "spx", None),
        P("orb", "spx"),
        P("orb"),
        P("orb", None),
        P("spx", None),
        P("spx", None),
    )
    return jax.shard_map(
        local, mesh=mesh, in_specs=placed, out_specs=(P("orb"), P("spx", None)), check_vma=False
    )
```

time: 48 us -> 51.3 us (1.069)
  Pallas kernels: 38.6 us -> 42 us
    pallas_call x1, Pallas kernels: 38.6 us -> 42 us  [local(): pl.pallas_call(functools.partial(kernel, n, m, velocity_bins, orbits // b...]
where the time goes in v1:
time: 51.3 us; the launch traced here: 50.9 us
  Pallas kernels  42 us (82%)
  local copies, waits for them, and re-layouts  8.32 us (16%)
  between operations  0.66 us (1%)
    pallas_call x1, Pallas kernels, local(): pl.pallas_call(functools.partial(kernel, n, m, velocity_bins, orbits // b...  42 us
    unnamed x16, local copies, waits for them, and re-layouts  8.32 us

profile of v1, /device:TPU:0, one launch (start us, length us, event | category | flops | bytes accessed | tf_op | source)
XLA Modules:
  0.0 50.9 jit_solution(15422798447799750467)
XLA Ops:
  0.6 0.0 copy-start
  0.6 2.2 %copy-done = bf16[4096,8,64]{0,2,1:T(8,128)(2,1)S(1)} copy-done((bf16[4096,8,64]{0,2,1:T(8,128)(2,1)S(1)}, bf16[4096,8,64]{0,2,1:T(8,128)(2,1)}, u32[]{:S(2)}) %copy-start) | copy-done | bytes 4194328
  2.8 0.0 copy-start.1
  2.8 1.0 %copy-done.1 = bf16[32,4160]{1,0:T(8,128)(2,1)S(1)} copy-done((bf16[32,4160]{1,0:T(8,128)(2,1)S(1)}, bf16[32,4160]{1,0:T(8,128)(2,1)}, u32[]{:S(2)}) %copy-start.1) | copy-done | bytes 266264
  3.8 0.0 copy-start.2
  3.8 0.9 %copy-done.2 = f32[8,4096]{1,0:T(8,128)S(1)} copy-done((f32[8,4096]{1,0:T(8,128)S(1)}, f32[8,4096]{1,0:T(8,128)}, u32[]{:S(2)}) %copy-start.2) | copy-done | bytes 131096
  4.7 0.0 copy-start.3
  4.7 0.9 %copy-done.3 = f32[8,4096]{1,0:T(8,128)S(1)} copy-done((f32[8,4096]{1,0:T(8,128)S(1)}, f32[8,4096]{1,0:T(8,128)}, u32[]{:S(2)}) %copy-start.3) | copy-done | bytes 131096
  5.6 0.0 copy-start.4
  5.6 0.7 %copy-done.4 = f32[4096]{0:T(1024)S(1)} copy-done((f32[4096]{0:T(1024)S(1)}, f32[4096]{0:T(1024)}, u32[]{:S(2)}) %copy-start.4) | copy-done | bytes 16408
  6.3 0.0 copy-start.5
  6.3 0.7 %copy-done.5 = s32[4096]{0:T(1024)S(1)} copy-done((s32[4096]{0:T(1024)S(1)}, s32[4096]{0:T(1024)}, u32[]{:S(2)}) %copy-start.5) | copy-done | bytes 16408
  7.0 0.0 copy-start.6
  7.0 0.7 %copy-done.6 = s32[32,8]{0,1:T(8,128)S(1)} copy-done((s32[32,8]{0,1:T(8,128)S(1)}, s32[32,8]{0,1:T(8,128)}, u32[]{:S(2)}) %copy-start.6) | copy-done | bytes 1048
  7.7 42.0 %shard_map.86 = (f32[1,4096]{1,0:T(1,128)S(1)}, f32[8,4096]{1,0:T(8,128)S(1)}) custom-call(f32[1,4096]{1,0:T(1,128)S(1)} %bitcast.8, bf16[512,4096]{1,0:T(8,128)(2,1)S(1)} %bitcast.7, s32[8,32]{1,0:T(8,128)S(1)} %bitcast.11, s32[1,4096]{1,0:T(1,128)S(1)} %bitcast.9, bf16[32,4160]{1,0:T(8,128)(2,1)S(1)} %copy-done.1, f32[8,4096]{1,0:T(8,128)S(1)} %copy-done.2, ...), custom_call_target="tpu_custom_call" | custom-call | tf_op jit(solution)/shard_map/pallas_call | solution.py:328
  49.7 0.6 %copy.11 = f32[4096]{0:T(1024)} copy(f32[4096]{0:T(1024)S(1)} %bitcast.10) | data formatting | bytes 32768
  50.3 0.7 %copy.12 = f32[8,4096]{1,0:T(8,128)} copy(f32[8,4096]{1,0:T(8,128)S(1)} %get-tuple-element.9) | data formatting | bytes 262144
Async XLA Ops:
  0.6 2.2 %copy-start = (bf16[4096,8,64]{0,2,1:T(8,128)(2,1)S(1)}, bf16[4096,8,64]{0,2,1:T(8,128)(2,1)}, u32[]{:S(2)}) copy-start(bf16[4096,8,64]{0,2,1:T(8,128)(2,1)} %param.8) | copy-start | bytes 12582916
  2.8 1.0 %copy-start.1 = (bf16[32,4160]{1,0:T(8,128)(2,1)S(1)}, bf16[32,4160]{1,0:T(8,128)(2,1)}, u32[]{:S(2)}) copy-start(bf16[32,4160]{1,0:T(8,128)(2,1)} %t_hbm.1) | copy-start | bytes 798724
  3.8 0.9 %copy-start.2 = (f32[8,4096]{1,0:T(8,128)S(1)}, f32[8,4096]{1,0:T(8,128)}, u32[]{:S(2)}) copy-start(f32[8,4096]{1,0:T(8,128)} %obs_hbm.1) | copy-start | bytes 393220
  4.7 0.9 %copy-start.3 = (f32[8,4096]{1,0:T(8,128)S(1)}, f32[8,4096]{1,0:T(8,128)}, u32[]{:S(2)}) copy-start(f32[8,4096]{1,0:T(8,128)} %inv_hbm.1) | copy-start | bytes 393220
  5.6 0.7 %copy-start.4 = (f32[4096]{0:T(1024)S(1)}, f32[4096]{0:T(1024)}, u32[]{:S(2)}) copy-start(f32[4096]{0:T(1024)} %param.7) | copy-start | bytes 49156
  6.3 0.7 %copy-start.5 = (s32[4096]{0:T(1024)S(1)}, s32[4096]{0:T(1024)}, u32[]{:S(2)}) copy-start(s32[4096]{0:T(1024)} %param.10) | copy-start | bytes 49156
  7.0 0.7 %copy-start.6 = (s32[32,8]{0,1:T(8,128)S(1)}, s32[32,8]{0,1:T(8,128)}, u32[]{:S(2)}) copy-start(s32[32,8]{0,1:T(8,128)} %param.9) | copy-start | bytes 3076

commit v2 on v1

--- a/solution.py
+++ b/solution.py
@@ -319,7 +319,7 @@
     oc = min(512, orbits)
     chunks = orbits // oc
     wide = waves + -(-(twaves - waves) // 128) * 128
-    halves = groups = 2
+    halves = groups = 1
     half = rows // halves
     chips = n // 2
     coarse = velocity_bins // fine
@@ -356,7 +356,7 @@
             dma((groups, m)), dma((groups, m)),
         ],
         compiler_params=pltpu.CompilerParams(
-            collective_id=0, has_side_effects=True, vmem_limit_bytes=48 * 2**20),
+            collective_id=0, has_side_effects=True, vmem_limit_bytes=60 * 2**20),
     )(
         weights.reshape(1, orbits),
         jnp.transpose(losvd, (1, 2, 0)).reshape(rows, orbits),

time: 51.3 us -> 45.5 us (0.89)
  local copies, waits for them, and re-layouts: 8.32 us -> 2.89 us
    unnamed x16 -> x2, local copies, waits for them, and re-layouts: 8.32 us -> 2.89 us
where the time goes in v2:
time: 45.5 us; the launch traced here: 45.3 us
  Pallas kernels  41.8 us (92%)
  local copies, waits for them, and re-layouts  2.89 us (6%)
  between operations  0.64 us (1%)
    pallas_call x1, Pallas kernels, local(): pl.pallas_call(functools.partial(kernel, n, m, velocity_bins, orbits // b...  41.8 us
    unnamed x2, local copies, waits for them, and re-layouts  2.89 us

profile of v2, /device:TPU:0, one launch (start us, length us, event | category | flops | bytes accessed | tf_op | source)
XLA Modules:
  0.0 45.3 jit_solution(2055657290039817548)
XLA Ops:
  0.6 41.8 %shard_map.86 = (f32[1,4096]{1,0:T(1,128)}, f32[8,4096]{1,0:T(8,128)}) custom-call(f32[1,4096]{1,0:T(1,128)} %bitcast.8, bf16[512,4096]{1,0:T(8,128)(2,1)} %bitcast.7, s32[8,32]{1,0:T(8,128)} %bitcast.11, s32[1,4096]{1,0:T(1,128)} %bitcast.9, bf16[32,4160]{1,0:T(8,128)(2,1)} %t_hbm.1, f32[8,4096]{1,0:T(8,128)} %obs_hbm.1, f32[8,4096]{1,0:T(8,128)} %inv_hbm.1), custom_call_target="tpu_custom_call" | custom-call | tf_op jit(solution)/shard_map/pallas_call | solution.py:328
  42.4 1.3 %copy.11 = f32[4096]{0:T(1024)} copy(f32[4096]{0:T(1024)} %bitcast.10) | data formatting | bytes 32768
  43.7 1.6 %copy.12 = f32[8,4096]{1,0:T(8,128)} copy(f32[8,4096]{1,0:T(8,128)} %get-tuple-element.9) | data formatting | bytes 262144
